TPU v7x, 32 devices: a whole 2x2x4 slice. The times are simulated.
32 devices in a mesh: vp: 8 (over z, x), vc: 4 (over y, core).
Axes of the slice: x: 2, y: 2, z: 4, core: 2. Of those that a mesh axis runs over, the one named last changes fastest.
Arguments:
- amplitudes: bfloat16 [64, 102400], P(('vp', 'vc')), may hold values from -6 to 6
- pair_tiles: bfloat16 [8192, 128, 128], P(('vp', 'vc')), may hold values from -0.09375 to 0.09375
- slot_pairs: int32 [8192, 2], P(('vp', 'vc')), may hold values from 0 to 199, as said below
- slot_count: int32 [32], P(('vp', 'vc')), may hold values from 32 to 256, as said below
Outputs:
- ladder: bfloat16 [64, 16384], P('vc', 'vp')
Inputs may be any that keep to these rules, and one draw needn't show every extreme that they name: `slot_pairs`: the rows of one device name distinct pairs; column 0 lies in 0 to 15, column 1 in 0 to 199. `slot_count`: every count is 256 divided by 1, 2, 4 or 8; some device has exactly 256.
All inputs are finite; a program needn't handle non-finite values.
Results may differ from a plain program's by a relative error of at most 0.001.
Values may be sent and summed in bfloat16 or wider, within the bound.
A program may use at most 128 MiB of HBM per device.

v0:
```python
import functools
import math

import jax
import jax.numpy as jnp
from jax import lax
from jax.experimental import pallas as pl
from jax.experimental.pallas import tpu as pltpu
from jax.sharding import PartitionSpec as P

AB_TILES = 16
SLOW = 4
VMEM = 60 * 1024 * 1024
MESH = pl.DeviceIdType.MESH


def largest_divisor(value, limit):
    return max(d for d in range(1, limit + 1) if value % d == 0)


def gather(dims, amp_ref, full_ref, pieces, piece_send, piece_recv,
           up_send, down_send, chain_recv, side_send, side_recv, meanwhile):
    slow, fast, vcs, tiles, shared, size = dims
    share = (tiles - shared) // fast
    held = share + shared
    own_chunks, chunks = share // size, held // size
    group = fast * vcs
    vp = lax.axis_index("vp")
    c = lax.axis_index("vc")
    a, b = lax.div(vp, fast), lax.rem(vp, fast)
    me = b * vcs + c

    def in_plane(step):
        other = lax.rem(me + step, group)
        return lax.div(other, vcs), lax.rem(other, vcs)

    def plane_id(ob, oc):
        return (a * fast + ob, oc)

    def tile_at(ob, k):
        return jnp.where(k < own_chunks, ob * share + k * size, fast * share + (k - own_chunks) * size)

    barrier = pltpu.get_barrier_semaphore()

    def greet(step, carry):
        ob, oc = in_plane(step)
        pl.semaphore_signal(barrier, inc=1, device_id=plane_id(ob, oc), device_id_type=MESH)
        return carry

    lax.fori_loop(1, group, greet, 0)

    @pl.when(a > 0)
    def _():
        pl.semaphore_signal(barrier, inc=1, device_id=(vp - fast, c), device_id_type=MESH)

    @pl.when(a < slow - 1)
    def _():
        pl.semaphore_signal(barrier, inc=1, device_id=(vp + fast, c), device_id_type=MESH)

    edges = (a > 0).astype(jnp.int32) + (a < slow - 1).astype(jnp.int32)
    pl.semaphore_wait(barrier, group - 1 + edges)

    def send_pieces(k, carry):
        def one(step, carry):
            ob, oc = in_plane(step)
            pltpu.make_async_remote_copy(
                src_ref=amp_ref.at[pl.ds(oc * tiles + tile_at(ob, k), size)],
                dst_ref=pieces.at[me, pl.ds(k * size, size)],
                send_sem=piece_send, recv_sem=piece_recv.at[k],
                device_id=plane_id(ob, oc), device_id_type=MESH).start()
            return carry
        return lax.fori_loop(1, group, one, carry)

    ahead = min(2, chunks)
    lax.fori_loop(0, ahead, send_pieces, 0)
    pieces[me, :share] = amp_ref[pl.ds(c * tiles + b * share, share)]
    if shared:
        pieces[me, share:] = amp_ref[pl.ds(c * tiles + fast * share, shared)]

    meanwhile()

    def block(plane, k):
        return full_ref.at[plane, pl.ds(tile_at(b, k), size)]

    def up(plane, k):
        return pltpu.make_async_remote_copy(
            src_ref=block(plane, k), dst_ref=block(plane, k),
            send_sem=up_send.at[plane, k], recv_sem=chain_recv.at[plane, k],
            device_id=(vp + fast, c), device_id_type=MESH)

    def down(plane, k):
        return pltpu.make_async_remote_copy(
            src_ref=block(plane, k), dst_ref=block(plane, k),
            send_sem=down_send.at[plane, k], recv_sem=chain_recv.at[plane, k],
            device_id=(vp - fast, c), device_id_type=MESH)

    def sideways(plane, k):
        def one(step, carry):
            ob = lax.rem(b + step, fast)
            pltpu.make_async_remote_copy(
                src_ref=block(plane, k), dst_ref=block(plane, k),
                send_sem=side_send, recv_sem=side_recv,
                device_id=plane_id(ob, c), device_id_type=MESH).start()
            return carry
        lax.fori_loop(1, fast, one, 0)

    def own_chunk(k, side):
        arrived = pieces.at[pl.ds(0, group - 1), pl.ds(k * size, size)]
        pltpu.make_async_copy(arrived, arrived, piece_recv.at[k]).wait()
        full_ref[a, pl.ds(tile_at(b, k), size)] = jnp.concatenate(
            [pieces[i, pl.ds(k * size, size)] for i in range(group)], axis=1)

        @pl.when(a > 0)
        def _():
            down(a, k).start()

        @pl.when(a < slow - 1)
        def _():
            up(a, k).start()

        if side:
            sideways(a, k)

        @pl.when(k + ahead < chunks)
        def _():
            send_pieces(k + ahead, 0)

    def passed_chunk(far, k, side):
        @pl.when(a - far >= 0)
        def _():
            up(a - far, k).wait_recv()

            @pl.when(a < slow - 1)
            def _():
                up(a - far, k).start()

            if side:
                sideways(a - far, k)

        @pl.when(a + far < slow)
        def _():
            down(a + far, k).wait_recv()

            @pl.when(a > 0)
            def _():
                down(a + far, k).start()

            if side:
                sideways(a + far, k)

    for first, last, side in ((0, own_chunks, True), (own_chunks, chunks, False)):
        if first == last:
            continue

        def own(k, carry, side=side):
            own_chunk(k, side)
            return carry

        lax.fori_loop(first, last, own, 0)
        for far in range(1, slow):
            def passed(k, carry, far=far, side=side):
                passed_chunk(far, k, side)
                return carry

            lax.fori_loop(first, last, passed, 0)

    if fast > 1:
        moved = full_ref.at[:, pl.ds(0, (fast - 1) * share)]
        pltpu.make_async_copy(moved, moved, side_recv).wait()


def gather_sends(dims, full_ref, pieces, piece_send, up_send, down_send, side_send):
    slow, fast, vcs, tiles, shared, size = dims
    share = (tiles - shared) // fast
    chunks = (share + shared) // size
    group = fast * vcs
    a = lax.div(lax.axis_index("vp"), fast)
    one = full_ref.at[0, pl.ds(0, size)]
    if fast > 1:
        moved = full_ref.at[:, pl.ds(0, (fast - 1) * share)]
        pltpu.make_async_copy(moved, moved, side_send).wait()
    sent = pieces.at[pl.ds(0, group - 1)]
    pltpu.make_async_copy(sent, sent, piece_send).wait()

    for far in range(slow):
        def sent_chunk(k, carry, far=far):
            @pl.when((a - far >= 0) & (a < slow - 1))
            def _():
                pltpu.make_async_copy(one, one, up_send.at[a - far, k]).wait()

            @pl.when((a + far < slow) & (a > 0))
            def _():
                pltpu.make_async_copy(one, one, down_send.at[a + far, k]).wait()

            return carry

        lax.fori_loop(0, chunks, sent_chunk, 0)


def sum_partials(pair, pieces, part_ref, out_ref, near, sums, far, near_send, near_recv, far_send, far_recv):
    parts, ab_tiles, _, width = part_ref.shape
    outer = parts // pair
    size = ab_tiles // pieces
    c = lax.axis_index("vc")
    vp = lax.axis_index("vp")
    y, core = lax.div(c, pair), lax.rem(c, pair)

    def other_y(step):
        return lax.rem(y + step, outer)

    steps = list(range(1, outer)) + [0]
    waits = []
    nears = {}
    if pair == 2:
        for step in steps:
            i = other_y(step)
            for h in range(pieces):
                copy = pltpu.make_async_remote_copy(
                    src_ref=part_ref.at[i * pair + 1 - core, pl.ds(h * size, size)],
                    dst_ref=near.at[i, pl.ds(h * size, size)],
                    send_sem=near_send.at[step, h], recv_sem=near_recv.at[step, h],
                    device_id=(vp, y * pair + 1 - core), device_id_type=MESH)
                copy.start()
                nears[step, h] = copy
                waits.append(copy)

    def chip_sum(step, h):
        i = other_y(step)
        window = pl.ds(h * size, size)
        value = part_ref[i * pair + core, window]
        if pair == 2:
            nears[step, h].wait_recv()
            value = value + near[i, window]
        return i, window, value

    fars = {}
    for h in range(pieces):
        for step in steps[:-1]:
            i, window, value = chip_sum(step, h)
            sums[i, window] = value
            copy = pltpu.make_async_remote_copy(
                src_ref=sums.at[i, window], dst_ref=far.at[step - 1, window],
                send_sem=far_send.at[step - 1, h], recv_sem=far_recv.at[step - 1, h],
                device_id=(vp, i * pair + core), device_id_type=MESH)
            copy.start()
            fars[step, h] = copy
            waits.append(copy)
    for h in range(pieces):
        _, window, total = chip_sum(0, h)
        for step in steps[:-1]:
            fars[step, h].wait_recv()
            total = total + far[step - 1, window]
        for n in range(size):
            at = (h * size + n) * width
            out_ref[:, at:at + width] = total[n].astype(out_ref.dtype)
    for copy in waits:
        copy.wait_send()


def sort_slots(count, pairs_ref, table):
    slots = pairs_ref.shape[1]
    ab_row = pairs_ref[0:1, :]
    rows = lax.broadcasted_iota(jnp.int32, (slots, slots), 0)
    lanes = lax.broadcasted_iota(jnp.int32, (slots, slots), 1)

    def as_column(row):
        return jnp.sum(jnp.where(rows == lanes, row, 0), axis=1, keepdims=True)

    slot_row = lax.broadcasted_iota(jnp.int32, (1, slots), 1)
    key_row = jnp.where(slot_row < count, ab_row, AB_TILES) * slots + slot_row
    key_col = as_column(key_row)
    rank_col = jnp.sum((key_row < key_col).astype(jnp.int32), axis=1, keepdims=True)
    chosen = rank_col == lanes

    def in_order(column):
        return jnp.sum(jnp.where(chosen, column, 0), axis=0, keepdims=True)

    table[...] = jnp.zeros_like(table)
    table[0:1, :] = in_order(rows[:, 0:1])
    table[1:2, :] = in_order(as_column(pairs_ref[1:2, :]))
    key_sorted = in_order(key_col)
    same = jnp.any((rank_col + 1 == lanes) & (lax.div(key_col, slots) == lax.div(key_sorted, slots)),
                   axis=0, keepdims=True)
    table[2:3, :] = same.astype(jnp.int32)
    table[3:4, :] = jnp.sum((key_col < (lanes + 1) * slots).astype(jnp.int32), axis=0, keepdims=True)


def multiply(planes, first_row, row_count, batch, smem, full_ref, tiles, running):
    slots, width = tiles.shape[0], tiles.shape[1]
    rows = planes.size * row_count

    def step(j, total):
        base = j * batch
        products = []
        for n in range(batch):
            left = full_ref[planes, smem[1, base + n], pl.ds(first_row, row_count)]
            products.append(jnp.dot(left.reshape(rows, width), tiles[smem[0, base + n]],
                                    preferred_element_type=jnp.float32))
        for n in range(batch):
            total = total * smem[2, base + n].astype(jnp.float32) + products[n]
            running[base + n] = total
        return total

    lax.fori_loop(0, slots // batch, step, jnp.zeros((rows, width), jnp.float32))


def last_totals(ab, smem, running):
    end = smem[3, ab]
    start = smem[3, ab - 1] if ab else 0
    some = jnp.minimum(end - start, 1).astype(jnp.float32)
    return running[jnp.maximum(end - 1, 0)] * some


def ladder_kernel(dims, batch, pieces_n, pair, count_ref, pairs_ref, amp_ref, tiles_hbm, out_ref,
                  full, pieces, tiles, running, partial, near, sums, far, table, smem,
                  piece_send, piece_recv, up_send, down_send, chain_recv, side_send, side_recv,
                  tile_sem, table_sem, near_send, near_recv, far_send, far_recv):
    slow, plane_rows = full.shape[0], full.shape[2]
    out_rows = partial.shape[2]
    width = tiles.shape[2]

    def meanwhile():
        pltpu.make_async_copy(tiles_hbm, tiles, tile_sem).start()
        sort_slots(count_ref[0], pairs_ref, table)
        pltpu.make_async_copy(table, smem, table_sem).start()

    gather(dims, amp_ref, full, pieces, piece_send, piece_recv,
           up_send, down_send, chain_recv, side_send, side_recv, meanwhile)
    pltpu.make_async_copy(tiles_hbm, tiles, tile_sem).wait()
    pltpu.make_async_copy(table, smem, table_sem).wait()

    at_once = running.shape[1]
    row_count = min(at_once, plane_rows)
    planes = at_once // row_count
    for plane in range(0, slow, planes):
        for row in range(0, plane_rows, row_count):
            multiply(pl.ds(plane, planes), row, row_count, batch, smem, full, tiles, running)
            target = (plane * plane_rows + row) // out_rows
            for ab in range(AB_TILES):
                partial[target:target + at_once // out_rows, ab] = last_totals(
                    ab, smem, running).reshape(at_once // out_rows, out_rows, width)

    sum_partials(pair, pieces_n, partial, out_ref, near, sums, far, near_send, near_recv, far_send, far_recv)
    gather_sends(dims, full, pieces, piece_send, up_send, down_send, side_send)


def per_device(n_vp, n_vc, amplitudes, pair_tiles, slot_pairs, slot_count):
    own_rows, columns = amplitudes.shape
    slots, width, _ = pair_tiles.shape
    slow = SLOW if n_vp % SLOW == 0 else n_vp
    fast = n_vp // slow
    tiles = columns // width // n_vc
    rows = own_rows * n_vp * n_vc
    plane_rows = rows // slow
    shared = tiles // 5
    shared += (tiles - shared) % fast
    share = (tiles - shared) // fast
    size = largest_divisor(math.gcd(share, shared), 20)
    chunks = (share + shared) // size
    group = fast * n_vc
    in_vmem = pl.BlockSpec(memory_space=pltpu.VMEM)

    amp = amplitudes.reshape(own_rows, columns // width, width).transpose(1, 0, 2)
    out_rows = rows // n_vc
    at_once = min(rows, 64)
    slots_batch = largest_divisor(slots, 16)
    pair = 2 if n_vc % 2 == 0 else 1
    outer = n_vc // pair
    parts = largest_divisor(AB_TILES, 4)
    block = (AB_TILES, out_rows, width)
    dma = pltpu.SemaphoreType.DMA
    in_smem = pl.BlockSpec(memory_space=pltpu.SMEM)
    return pl.pallas_call(
        functools.partial(
            ladder_kernel, (slow, fast, n_vc, tiles, shared, size), slots_batch, parts, pair),
        out_shape=jax.ShapeDtypeStruct((out_rows, AB_TILES * width), jnp.bfloat16),
        in_specs=[in_smem, in_vmem, in_vmem, pl.BlockSpec(memory_space=pl.ANY)],
        out_specs=in_vmem,
        scratch_shapes=[
            pltpu.VMEM((slow, tiles, plane_rows, width), amplitudes.dtype),
            pltpu.VMEM((group, share + shared, own_rows, width), amplitudes.dtype),
            pltpu.VMEM(pair_tiles.shape, pair_tiles.dtype),
            pltpu.VMEM((slots, at_once, width), jnp.float32),
            pltpu.VMEM((n_vc,) + block, jnp.float32),
            pltpu.VMEM((outer,) + block, jnp.float32),
            pltpu.VMEM((outer,) + block, jnp.float32),
            pltpu.VMEM((max(outer - 1, 1),) + block, jnp.float32),
            pltpu.VMEM((8, slots), jnp.int32),
            pltpu.SMEM((8, slots), jnp.int32),
            dma, dma((chunks,)),
            dma((slow, chunks)), dma((slow, chunks)), dma((slow, chunks)),
            dma, dma, dma, dma,
            dma((outer, parts)), dma((outer, parts)), dma((outer, parts)), dma((outer, parts)),
        ],
        compiler_params=pltpu.CompilerParams(
            collective_id=0, has_side_effects=True, vmem_limit_bytes=VMEM),
        name="ladder",
    )(slot_count, slot_pairs.T, amp, pair_tiles)


def solution(mesh):
    in_specs = (
        P(("vp", "vc"), None),
        P(("vp", "vc"), None, None),
        P(("vp", "vc"), None),
        P(("vp", "vc")),
    )
    return jax.shard_map(
        functools.partial(per_device, mesh.shape["vp"], mesh.shape["vc"]),
        mesh=mesh, in_specs=in_specs, out_specs=P("vc", "vp"), check_vma=False)
```

profile of v0, /device:TPU:1, one launch (start us, length us, event | category | flops | bytes accessed | tf_op | source)
XLA Modules:
  0.0 60.6 jit_solution(8210757327993429640)
XLA Ops:
  0.7 58.5 %ladder.1 = bf16[16,2048]{1,0:T(8,128)(2,1)} custom-call(s32[1]{0:T(128)S(6)} %copy.6.count_ref, s32[2,256]{1,0:T(2,128)} %bitcast.5, bf16[800,2,128]{2,1,0:T(2,128)(2,1)} %bitcast.4, bf16[256,128,128]{2,1,0:T(8,128)(2,1)} %tiles_hbm.1), custom_call_target="tpu_custom_call" | custom-call | tf_op jit(solution)/shard_map/ladder/pallas_call | solution.py:373
  59.1 1.5 %copy.7 = bf16[16,2048]{1,0:T(8,128)(2,1)} copy(bf16[16,2048]{1,0:T(8,128)(2,1)} %ladder.1) | data formatting | bytes 131072
where the time goes:
time: 61 us; the launch traced here: 60.6 us
  Pallas kernels  58.5 us (96%)
  local copies, waits for them, and re-layouts  1.47 us (2%)
  between operations  0.66 us (1%)
    pallas_call x1, Pallas kernels, per_device(): pl.pallas_call(functools.partial(ladder_kernel, (slow, fast, n_vc, tiles,...  58.5 us
    unnamed x1, local copies, waits for them, and re-layouts  1.47 us

commit v1 on v0

v1 whole, which is shorter than its diff:
```python
import functools
import math

import jax
import jax.numpy as jnp
from jax import lax
from jax.experimental import pallas as pl
from jax.experimental.pallas import tpu as pltpu
from jax.sharding import PartitionSpec as P

AB_TILES = 16
SLOW = 4
PAIR = 2
VMEM = 60 * 1024 * 1024
MESH = pl.DeviceIdType.MESH


def largest_divisor(value, limit):
    return max(d for d in range(1, limit + 1) if value % d == 0)


def gather(dims, amp_ref, full_ref, late_ref, pieces, piece_send, piece_recv,
           up_send, down_send, chain_recv, side_send, side_recv, meanwhile):
    slow, fast, vcs, tiles, shared, size = dims
    share = (tiles - shared) // fast
    held = share + shared
    own_chunks, chunks = share // size, held // size
    group = fast * vcs
    vp = lax.axis_index("vp")
    c = lax.axis_index("vc")
    a, b = lax.div(vp, fast), lax.rem(vp, fast)
    me = b * vcs + c

    def in_plane(step):
        other = lax.rem(me + step, group)
        return lax.div(other, vcs), lax.rem(other, vcs)

    def plane_id(ob, oc):
        return (a * fast + ob, oc)

    def tile_at(ob, k):
        return jnp.where(k < own_chunks, ob * share + k * size, fast * share + (k - own_chunks) * size)

    barrier = pltpu.get_barrier_semaphore()

    def greet(step, carry):
        ob, oc = in_plane(step)
        pl.semaphore_signal(barrier, inc=1, device_id=plane_id(ob, oc), device_id_type=MESH)
        return carry

    lax.fori_loop(1, group, greet, 0)

    @pl.when(a > 0)
    def _():
        pl.semaphore_signal(barrier, inc=1, device_id=(vp - fast, c), device_id_type=MESH)

    @pl.when(a < slow - 1)
    def _():
        pl.semaphore_signal(barrier, inc=1, device_id=(vp + fast, c), device_id_type=MESH)

    edges = (a > 0).astype(jnp.int32) + (a < slow - 1).astype(jnp.int32)
    pl.semaphore_wait(barrier, group - 1 + edges)

    def send_pieces(k, carry):
        def one(step, carry):
            ob, oc = in_plane(step)
            pltpu.make_async_remote_copy(
                src_ref=amp_ref.at[pl.ds(oc * tiles + tile_at(ob, k), size)],
                dst_ref=pieces.at[me, pl.ds(k * size, size)],
                send_sem=piece_send, recv_sem=piece_recv.at[k],
                device_id=plane_id(ob, oc), device_id_type=MESH).start()
            return carry
        return lax.fori_loop(1, group, one, carry)

    ahead = min(2, chunks)
    lax.fori_loop(0, ahead, send_pieces, 0)
    pieces[me, :share] = amp_ref[pl.ds(c * tiles + b * share, share)]
    if shared:
        pieces[me, share:] = amp_ref[pl.ds(c * tiles + fast * share, shared)]

    def start_copy(plane, k, from_a, to_a, send_sem, recv_sem, device):
        window = pl.ds(tile_at(b, k), size)
        from_late, to_late = plane == last_plane(from_a, slow), plane == last_plane(to_a, slow)

        def place(is_late, at_a):
            return late_ref.at[window] if is_late else full_ref.at[plane - first_plane(at_a, slow), window]

        for source in (False, True):
            for target in (False, True):
                @pl.when((from_late == source) & (to_late == target))
                def _(source=source, target=target):
                    pltpu.make_async_remote_copy(
                        src_ref=place(source, from_a), dst_ref=place(target, to_a),
                        send_sem=send_sem, recv_sem=recv_sem,
                        device_id=device, device_id_type=MESH).start()

    def up(plane, k):
        start_copy(plane, k, a, a + 1, up_send.at[plane, k], chain_recv.at[plane, k], (vp + fast, c))

    def down(plane, k):
        start_copy(plane, k, a, a - 1, down_send.at[plane, k], chain_recv.at[plane, k], (vp - fast, c))

    def arrived(plane, k):
        one = late_ref.at[pl.ds(0, size)]
        pltpu.make_async_copy(one, one, chain_recv.at[plane, k]).wait()

    def sideways(plane, k):
        window = pl.ds(tile_at(b, k), size)
        is_late = plane == last_plane(a, slow)

        def one(step, carry):
            ob = lax.rem(b + step, fast)

            @pl.when(is_late)
            def _():
                pltpu.make_async_remote_copy(
                    src_ref=late_ref.at[window], dst_ref=late_ref.at[window],
                    send_sem=side_send.at[1], recv_sem=side_recv.at[1],
                    device_id=plane_id(ob, c), device_id_type=MESH).start()

            @pl.when(jnp.logical_not(is_late))
            def _():
                place = full_ref.at[plane - first_plane(a, slow), window]
                pltpu.make_async_remote_copy(
                    src_ref=place, dst_ref=place,
                    send_sem=side_send.at[0], recv_sem=side_recv.at[0],
                    device_id=plane_id(ob, c), device_id_type=MESH).start()

            return carry

        lax.fori_loop(1, fast, one, 0)

    def own_chunk(k, side):
        landed = pieces.at[pl.ds(0, group - 1), pl.ds(k * size, size)]
        pltpu.make_async_copy(landed, landed, piece_recv.at[k]).wait()
        full_ref[a - first_plane(a, slow), pl.ds(tile_at(b, k), size)] = jnp.concatenate(
            [pieces[i, pl.ds(k * size, size)] for i in range(group)], axis=1)

        @pl.when(a > 0)
        def _():
            down(a, k)

        @pl.when(a < slow - 1)
        def _():
            up(a, k)

        if side:
            sideways(a, k)

        @pl.when(k + ahead < chunks)
        def _():
            send_pieces(k + ahead, 0)

    def passed_chunk(far, k, side):
        @pl.when(a - far >= 0)
        def _():
            arrived(a - far, k)

            @pl.when(a < slow - 1)
            def _():
                up(a - far, k)

            if side:
                sideways(a - far, k)

        @pl.when(a + far < slow)
        def _():
            arrived(a + far, k)

            @pl.when(a > 0)
            def _():
                down(a + far, k)

            if side:
                sideways(a + far, k)

    for first, last, side in ((0, own_chunks, True), (own_chunks, chunks, False)):
        if first == last:
            continue

        def own(k, carry, side=side):
            own_chunk(k, side)
            return carry

        lax.fori_loop(first, last, own, 0)
        if first == 0:
            meanwhile()
        for far in range(1, slow if side else slow - 1):
            def passed(k, carry, far=far, side=side):
                passed_chunk(far, k, side)
                return carry

            lax.fori_loop(first, last, passed, 0)

    if fast > 1:
        moved = full_ref.at[:, pl.ds(0, (fast - 1) * share)]
        pltpu.make_async_copy(moved, moved, side_recv.at[0]).wait()


def last_plane(a, slow):
    return jnp.where(2 * a < slow, slow - 1, 0)


def first_plane(a, slow):
    return jnp.where(2 * a < slow, 0, 1)


def gather_rest(dims, late_ref, chain_recv, side_recv):
    slow, fast, vcs, tiles, shared, size = dims
    share = (tiles - shared) // fast
    own_chunks, chunks = share // size, (share + shared) // size
    a = lax.div(lax.axis_index("vp"), fast)
    one = late_ref.at[pl.ds(0, size)]

    @pl.when((a == 0) | (a == slow - 1))
    def _():
        def arrived(k, carry):
            pltpu.make_async_copy(one, one, chain_recv.at[last_plane(a, slow), k]).wait()
            return carry

        lax.fori_loop(own_chunks, chunks, arrived, 0)

    if fast > 1:
        moved = late_ref.at[pl.ds(0, (fast - 1) * share)]
        pltpu.make_async_copy(moved, moved, side_recv.at[1]).wait()


def gather_sends(dims, full_ref, late_ref, pieces, piece_send, up_send, down_send, side_send):
    slow, fast, vcs, tiles, shared, size = dims
    share = (tiles - shared) // fast
    chunks = (share + shared) // size
    group = fast * vcs
    a = lax.div(lax.axis_index("vp"), fast)
    one = late_ref.at[pl.ds(0, size)]
    if fast > 1:
        moved = full_ref.at[:, pl.ds(0, (fast - 1) * share)]
        pltpu.make_async_copy(moved, moved, side_send.at[0]).wait()
        moved = late_ref.at[pl.ds(0, (fast - 1) * share)]
        pltpu.make_async_copy(moved, moved, side_send.at[1]).wait()
    sent = pieces.at[pl.ds(0, group - 1)]
    pltpu.make_async_copy(sent, sent, piece_send).wait()

    for far in range(slow):
        def sent_chunk(k, carry, far=far):
            @pl.when((a - far >= 0) & (a < slow - 1))
            def _():
                pltpu.make_async_copy(one, one, up_send.at[a - far, k]).wait()

            @pl.when((a + far < slow) & (a > 0))
            def _():
                pltpu.make_async_copy(one, one, down_send.at[a + far, k]).wait()

            return carry

        lax.fori_loop(0, chunks, sent_chunk, 0)


def sort_slots(count, pairs_ref, table):
    slots = pairs_ref.shape[1]
    ab_row = pairs_ref[0:1, :]
    rows = lax.broadcasted_iota(jnp.int32, (slots, slots), 0)
    lanes = lax.broadcasted_iota(jnp.int32, (slots, slots), 1)

    def as_column(row):
        return jnp.sum(jnp.where(rows == lanes, row, 0), axis=1, keepdims=True)

    slot_row = lax.broadcasted_iota(jnp.int32, (1, slots), 1)
    key_row = jnp.where(slot_row < count, ab_row, AB_TILES) * slots + slot_row
    key_col = as_column(key_row)
    rank_col = jnp.sum((key_row < key_col).astype(jnp.int32), axis=1, keepdims=True)
    chosen = rank_col == lanes

    def in_order(column):
        return jnp.sum(jnp.where(chosen, column, 0), axis=0, keepdims=True)

    table[...] = jnp.zeros_like(table)
    table[0:1, :] = in_order(rows[:, 0:1])
    table[1:2, :] = in_order(as_column(pairs_ref[1:2, :]))
    key_sorted = in_order(key_col)
    same = jnp.any((rank_col + 1 == lanes) & (lax.div(key_col, slots) == lax.div(key_sorted, slots)),
                   axis=0, keepdims=True)
    table[2:3, :] = same.astype(jnp.int32)
    table[3:4, :] = jnp.sum((key_col < (lanes + 1) * slots).astype(jnp.int32), axis=0, keepdims=True)


def multiply(load, plane, planes, row, rows, batch, smem, tiles, running, partial, plane_rows):
    slots, width = tiles.shape[0], tiles.shape[1]
    out_rows = partial.shape[2]
    height = planes * rows

    def step(j, total):
        base = j * batch
        products = []
        for n in range(batch):
            left = load(smem[1, base + n])
            products.append(jnp.dot(left.reshape(height, width), tiles[smem[0, base + n]],
                                    preferred_element_type=jnp.float32))
        for n in range(batch):
            total = total * smem[2, base + n].astype(jnp.float32) + products[n]
            running[base + n, :height] = total
        return total

    lax.fori_loop(0, slots // batch, step, jnp.zeros((height, width), jnp.float32))
    count = height // out_rows
    target = pl.ds(plane * (plane_rows // out_rows) + row // out_rows, count)
    for ab in range(AB_TILES):
        end = smem[3, ab]
        start = smem[3, ab - 1] if ab else 0
        some = jnp.minimum(end - start, 1).astype(jnp.float32)
        total = running[jnp.maximum(end - 1, 0), :height] * some
        partial[target, ab] = total.reshape(count, out_rows, width)


def ladder_kernel(dims, batch, parts, count_ref, pairs_ref, amp_ref, tiles_hbm, out_ref,
                  full, late_rows, pieces, tiles, running, partial, near, sums, far, table, smem,
                  piece_send, piece_recv, up_send, down_send, chain_recv, side_send, side_recv,
                  tile_sem, table_sem, near_send, near_recv, far_send, far_recv):
    slow, fast, vcs = dims[:3]
    plane_rows = full.shape[2]
    out_rows = partial.shape[2]
    width = tiles.shape[2]
    per_plane = plane_rows // out_rows
    outer = vcs // PAIR
    part = AB_TILES // parts
    vp = lax.axis_index("vp")
    c = lax.axis_index("vc")
    y, core = lax.div(c, PAIR), lax.rem(c, PAIR)
    late = last_plane(lax.div(vp, fast), slow)
    early = first_plane(lax.div(vp, fast), slow)

    def meanwhile():
        pltpu.make_async_copy(tiles_hbm, tiles, tile_sem).start()
        sort_slots(count_ref[0], pairs_ref, table)
        pltpu.make_async_copy(table, smem, table_sem).start()

    def window(h):
        return pl.ds(h * part, part)

    def near_copy(target, h):
        i = lax.div(target, PAIR)
        return pltpu.make_async_remote_copy(
            src_ref=partial.at[target, window(h)], dst_ref=near.at[i, window(h)],
            send_sem=near_send.at[i, h], recv_sem=near_recv.at[i, h],
            device_id=(vp, y * PAIR + 1 - core), device_id_type=MESH)

    def far_copy(i, h):
        return pltpu.make_async_remote_copy(
            src_ref=sums.at[i, window(h)], dst_ref=far.at[y, window(h)],
            send_sem=far_send.at[i, h], recv_sem=far_recv.at[y, h],
            device_id=(vp, i * PAIR + core), device_id_type=MESH)

    def to_core(target):
        @pl.when(lax.rem(target, PAIR) != core)
        def _():
            for h in range(parts):
                near_copy(target, h).start()

    def to_chip(target):
        i = lax.div(target, PAIR)

        @pl.when((lax.rem(target, PAIR) == core) & (i != y))
        def _():
            for h in range(parts):
                near_copy(target, h).wait_recv()
                sums[i, window(h)] = partial[target, window(h)] + near[i, window(h)]
                far_copy(i, h).start()

    def multiply_early():
        rows = running.shape[1]
        if rows >= (slow - 1) * plane_rows:
            multiply(lambda tile: full[:, tile], early, slow - 1, 0, plane_rows,
                     batch, smem, tiles, running, partial, plane_rows)
            return
        for p in range(slow - 1):
            for row in range(0, plane_rows, rows):
                multiply(lambda tile, p=p, row=row: full[p, tile, pl.ds(row, rows)], early + p, 1, row, rows,
                         batch, smem, tiles, running, partial, plane_rows)

    def multiply_late():
        rows = min(running.shape[1], plane_rows)
        for row in range(0, plane_rows, rows):
            multiply(lambda tile, row=row: late_rows[tile, pl.ds(row, rows)], late, 1, row, rows,
                     batch, smem, tiles, running, partial, plane_rows)

    gather(dims, amp_ref, full, late_rows, pieces, piece_send, piece_recv,
           up_send, down_send, chain_recv, side_send, side_recv, meanwhile)
    pltpu.make_async_copy(tiles_hbm, tiles, tile_sem).wait()
    pltpu.make_async_copy(table, smem, table_sem).wait()

    early_targets = [early * per_plane + n for n in range((slow - 1) * per_plane)]
    late_targets = [late * per_plane + n for n in range(per_plane)]
    multiply_early()
    for target in early_targets:
        to_core(target)
    gather_rest(dims, late_rows, chain_recv, side_recv)
    for target in early_targets:
        to_chip(target)
    multiply_late()
    for target in late_targets:
        to_core(target)
    for target in late_targets:
        to_chip(target)

    for h in range(parts):
        near_copy(c, h).wait_recv()
        total = partial[c, window(h)] + near[y, window(h)]
        for step in range(1, outer):
            source = lax.rem(y + step, outer)
            arrived = far.at[source, window(h)]
            pltpu.make_async_copy(arrived, arrived, far_recv.at[source, h]).wait()
            total = total + far[source, window(h)]
        for n in range(part):
            at = (h * part + n) * width
            out_ref[:, at:at + width] = total[n].astype(out_ref.dtype)

    for i in range(outer):
        for h in range(parts):
            near_copy(i * PAIR + 1 - core, h).wait_send()

            @pl.when(i != y)
            def _(i=i, h=h):
                far_copy(i, h).wait_send()

    gather_sends(dims, full, late_rows, pieces, piece_send, up_send, down_send, side_send)


def per_device(n_vp, n_vc, amplitudes, pair_tiles, slot_pairs, slot_count):
    own_rows, columns = amplitudes.shape
    slots, width, _ = pair_tiles.shape
    slow = SLOW if n_vp % SLOW == 0 else n_vp
    fast = n_vp // slow
    tiles = columns // width // n_vc
    rows = own_rows * n_vp * n_vc
    plane_rows = rows // slow
    shared = tiles // 5
    shared += (tiles - shared) % fast
    share = (tiles - shared) // fast
    size = largest_divisor(math.gcd(share, shared), 20)
    chunks = (share + shared) // size
    group = fast * n_vc
    in_vmem = pl.BlockSpec(memory_space=pltpu.VMEM)

    amp = amplitudes.reshape(own_rows, columns // width, width).transpose(1, 0, 2)
    out_rows = rows // n_vc
    early_rows = rows - plane_rows
    at_once = early_rows if early_rows <= 64 else min(plane_rows, 64)
    slots_batch = largest_divisor(slots, 16)
    outer = n_vc // PAIR
    parts = largest_divisor(AB_TILES, 4)
    block = (AB_TILES, out_rows, width)
    dma = pltpu.SemaphoreType.DMA
    in_smem = pl.BlockSpec(memory_space=pltpu.SMEM)
    return pl.pallas_call(
        functools.partial(
            ladder_kernel, (slow, fast, n_vc, tiles, shared, size), slots_batch, parts),
        out_shape=jax.ShapeDtypeStruct((out_rows, AB_TILES * width), jnp.bfloat16),
        in_specs=[in_smem, in_vmem, in_vmem, pl.BlockSpec(memory_space=pl.ANY)],
        out_specs=in_vmem,
        scratch_shapes=[
            pltpu.VMEM((slow - 1, tiles, plane_rows, width), amplitudes.dtype),
            pltpu.VMEM((tiles, plane_rows, width), amplitudes.dtype),
            pltpu.VMEM((group, share + shared, own_rows, width), amplitudes.dtype),
            pltpu.VMEM(pair_tiles.shape, pair_tiles.dtype),
            pltpu.VMEM((slots, at_once, width), jnp.float32),
            pltpu.VMEM((n_vc,) + block, jnp.float32),
            pltpu.VMEM((outer,) + block, jnp.float32),
            pltpu.VMEM((outer,) + block, jnp.float32),
            pltpu.VMEM((outer,) + block, jnp.float32),
            pltpu.VMEM((8, slots), jnp.int32),
            pltpu.SMEM((8, slots), jnp.int32),
            dma, dma((chunks,)),
            dma((slow, chunks)), dma((slow, chunks)), dma((slow, chunks)),
            dma((2,)), dma((2,)), dma, dma,
            dma((outer, parts)), dma((outer, parts)), dma((outer, parts)), dma((outer, parts)),
        ],
        compiler_params=pltpu.CompilerParams(
            collective_id=0, has_side_effects=True, vmem_limit_bytes=VMEM),
        name="ladder",
    )(slot_count, slot_pairs.T, amp, pair_tiles)


def solution(mesh):
    in_specs = (
        P(("vp", "vc"), None),
        P(("vp", "vc"), None, None),
        P(("vp", "vc"), None),
        P(("vp", "vc")),
    )
    return jax.shard_map(
        functools.partial(per_device, mesh.shape["vp"], mesh.shape["vc"]),
        mesh=mesh, in_specs=in_specs, out_specs=P("vc", "vp"), check_vma=False)
```

time: 61 us -> 59.7 us (0.979)
  Pallas kernels: 58.5 us -> 57.2 us
    pallas_call x1, Pallas kernels: 58.5 us -> 57.2 us  [per_device(): pl.pallas_call(functools.partial(ladder_kernel, (slow, fast, n_vc, tiles,...]
where the time goes in v1:
time: 59.7 us; the launch traced here: 59.3 us
  Pallas kernels  57.2 us (96%)
  local copies, waits for them, and re-layouts  1.47 us (2%)
  between operations  0.66 us (1%)
    pallas_call x1, Pallas kernels, per_device(): pl.pallas_call(functools.partial(ladder_kernel, (slow, fast, n_vc, tiles,...  57.2 us
    unnamed x1, local copies, waits for them, and re-layouts  1.47 us

profile of v1, /device:TPU:1, one launch (start us, length us, event | category | flops | bytes accessed | tf_op | source)
XLA Modules:
  0.0 59.3 jit_solution(17548340240388203418)
XLA Ops:
  0.7 57.2 %ladder.1 = bf16[16,2048]{1,0:T(8,128)(2,1)} custom-call(s32[1]{0:T(128)S(6)} %copy.6.count_ref, s32[2,256]{1,0:T(2,128)} %bitcast.5, bf16[800,2,128]{2,1,0:T(2,128)(2,1)} %bitcast.4, bf16[256,128,128]{2,1,0:T(8,128)(2,1)} %tiles_hbm.1), custom_call_target="tpu_custom_call" | custom-call | tf_op jit(solution)/shard_map/ladder/pallas_call | solution.py:453
  57.9 1.5 %copy.7 = bf16[16,2048]{1,0:T(8,128)(2,1)} copy(bf16[16,2048]{1,0:T(8,128)(2,1)} %ladder.1) | data formatting | bytes 131072

commit v2 on v1

--- a/solution.py
+++ b/solution.py
@@ -1,5 +1,4 @@
 import functools
-import math
 
 import jax
 import jax.numpy as jnp
@@ -24,6 +23,8 @@
     slow, fast, vcs, tiles, shared, size = dims
     share = (tiles - shared) // fast
     held = share + shared
+    height = amp_ref.shape[1]
+    unit = tiles * vcs // amp_ref.shape[0]
     own_chunks, chunks = share // size, held // size
     group = fast * vcs
     vp = lax.axis_index("vp")
@@ -65,18 +66,25 @@
         def one(step, carry):
             ob, oc = in_plane(step)
             pltpu.make_async_remote_copy(
-                src_ref=amp_ref.at[pl.ds(oc * tiles + tile_at(ob, k), size)],
-                dst_ref=pieces.at[me, pl.ds(k * size, size)],
+                src_ref=amp_ref.at[pl.ds(lax.div(oc * tiles + tile_at(ob, k), unit), size // unit)],
+                dst_ref=pieces.at[me, pl.ds(k * (size // unit), size // unit)],
                 send_sem=piece_send, recv_sem=piece_recv.at[k],
                 device_id=plane_id(ob, oc), device_id_type=MESH).start()
             return carry
         return lax.fori_loop(1, group, one, carry)
 
-    ahead = min(2, chunks)
+    ahead = min(4, chunks)
     lax.fori_loop(0, ahead, send_pieces, 0)
-    pieces[me, :share] = amp_ref[pl.ds(c * tiles + b * share, share)]
+    pieces[me, :share // unit] = amp_ref[pl.ds(lax.div(c * tiles + b * share, unit), share // unit)]
     if shared:
-        pieces[me, share:] = amp_ref[pl.ds(c * tiles + fast * share, shared)]
+        pieces[me, share // unit:] = amp_ref[pl.ds(lax.div(c * tiles + fast * share, unit), shared // unit)]
+
+    block = unit * height
+    to = lax.broadcasted_iota(jnp.int32, (block, block), 0)
+    at = lax.broadcasted_iota(jnp.int32, (block, block), 1)
+    own_rows = height // unit
+    source, tile, r = lax.div(lax.rem(to, height), own_rows), lax.div(to, height), lax.rem(to, own_rows)
+    order = (at == source * height + tile * own_rows + r).astype(jnp.float32).astype(amp_ref.dtype)
 
     def start_copy(plane, k, from_a, to_a, send_sem, recv_sem, device):
         window = pl.ds(tile_at(b, k), size)
@@ -131,10 +139,14 @@
         lax.fori_loop(1, fast, one, 0)
 
     def own_chunk(k, side):
-        landed = pieces.at[pl.ds(0, group - 1), pl.ds(k * size, size)]
+        landed = pieces.at[pl.ds(0, group - 1), pl.ds(k * (size // unit), size // unit)]
         pltpu.make_async_copy(landed, landed, piece_recv.at[k]).wait()
-        full_ref[a - first_plane(a, slow), pl.ds(tile_at(b, k), size)] = jnp.concatenate(
-            [pieces[i, pl.ds(k * size, size)] for i in range(group)], axis=1)
+        for n in range(size // unit):
+            for i in range(group // unit):
+                mixed = pieces[pl.ds(i * unit, unit), k * (size // unit) + n].reshape(block, -1)
+                sorted_rows = jnp.dot(order, mixed, preferred_element_type=jnp.float32).astype(amp_ref.dtype)
+                full_ref[a - first_plane(a, slow), pl.ds(tile_at(b, k) + n * unit, unit),
+                         pl.ds(i * height, height)] = sorted_rows.reshape(unit, height, -1)
 
         @pl.when(a > 0)
         def _():
@@ -432,15 +444,16 @@
     tiles = columns // width // n_vc
     rows = own_rows * n_vp * n_vc
     plane_rows = rows // slow
-    shared = tiles // 5
-    shared += (tiles - shared) % fast
-    share = (tiles - shared) // fast
-    size = largest_divisor(math.gcd(share, shared), 20)
+    unit = 16 // own_rows
+    share = (tiles - tiles // 5) // fast // unit * unit
+    shared = tiles - fast * share
+    size = unit
     chunks = (share + shared) // size
     group = fast * n_vc
     in_vmem = pl.BlockSpec(memory_space=pltpu.VMEM)
 
     amp = amplitudes.reshape(own_rows, columns // width, width).transpose(1, 0, 2)
+    amp = amp.reshape(-1, unit * own_rows, width)
     out_rows = rows // n_vc
     early_rows = rows - plane_rows
     at_once = early_rows if early_rows <= 64 else min(plane_rows, 64)
@@ -459,7 +472,7 @@
         scratch_shapes=[
             pltpu.VMEM((slow - 1, tiles, plane_rows, width), amplitudes.dtype),
             pltpu.VMEM((tiles, plane_rows, width), amplitudes.dtype),
-            pltpu.VMEM((group, share + shared, own_rows, width), amplitudes.dtype),
+            pltpu.VMEM((group, (share + shared) // unit, unit * own_rows, width), amplitudes.dtype),
             pltpu.VMEM(pair_tiles.shape, pair_tiles.dtype),
             pltpu.VMEM((slots, at_once, width), jnp.float32),
             pltpu.VMEM((n_vc,) + block, jnp.float32),

time: 59.7 us -> 67.8 us (1.14)
  Pallas kernels: 57.2 us -> 65.5 us
    pallas_call x1, Pallas kernels: 57.2 us -> 65.5 us  [per_device(): pl.pallas_call(functools.partial(ladder_kernel, (slow, fast, n_vc, tiles,...]
where the time goes in v2:
time: 67.8 us; the launch traced here: 67.6 us
  Pallas kernels  65.5 us (97%)
  local copies, waits for them, and re-layouts  1.47 us (2%)
    pallas_call x1, Pallas kernels, per_device(): pl.pallas_call(functools.partial(ladder_kernel, (slow, fast, n_vc, tiles,...  65.5 us
    unnamed x1, local copies, waits for them, and re-layouts  1.47 us

profile of v2, /device:TPU:1, one launch (start us, length us, event | category | flops | bytes accessed | tf_op | source)
XLA Modules:
  0.0 67.6 jit_solution(1032355606490001431)
XLA Ops:
  0.7 65.5 %ladder.1 = bf16[16,2048]{1,0:T(8,128)(2,1)} custom-call(s32[1]{0:T(128)S(6)} %copy.7.count_ref, s32[2,256]{1,0:T(2,128)} %bitcast.7, bf16[100,16,128]{2,1,0:T(8,128)(2,1)} %bitcast.6, bf16[256,128,128]{2,1,0:T(8,128)(2,1)} %tiles_hbm.1), custom_call_target="tpu_custom_call" | custom-call | tf_op jit(solution)/shard_map/ladder/pallas_call | solution.py:466
  66.2 1.5 %copy.8 = bf16[16,2048]{1,0:T(8,128)(2,1)} copy(bf16[16,2048]{1,0:T(8,128)(2,1)} %ladder.1) | data formatting | bytes 131072

commit v3 on v2

--- a/solution.py
+++ b/solution.py
@@ -1,4 +1,5 @@
 import functools
+import math
 
 import jax
 import jax.numpy as jnp
@@ -73,7 +74,7 @@
             return carry
         return lax.fori_loop(1, group, one, carry)
 
-    ahead = min(4, chunks)
+    ahead = min(2, chunks)
     lax.fori_loop(0, ahead, send_pieces, 0)
     pieces[me, :share // unit] = amp_ref[pl.ds(lax.div(c * tiles + b * share, unit), share // unit)]
     if shared:
@@ -447,7 +448,7 @@
     unit = 16 // own_rows
     share = (tiles - tiles // 5) // fast // unit * unit
     shared = tiles - fast * share
-    size = unit
+    size = math.gcd(share, shared)
     chunks = (share + shared) // size
     group = fast * n_vc
     in_vmem = pl.BlockSpec(memory_space=pltpu.VMEM)

time: 67.8 us -> 59.3 us (0.87)
  Pallas kernels: 65.5 us -> 57 us
    pallas_call x1, Pallas kernels: 65.5 us -> 57 us  [per_device(): pl.pallas_call(functools.partial(ladder_kernel, (slow, fast, n_vc, tiles,...]
where the time goes in v3:
time: 59.3 us; the launch traced here: 59.1 us
  Pallas kernels  57 us (96%)
  local copies, waits for them, and re-layouts  1.47 us (2%)
  between operations  0.66 us (1%)
    pallas_call x1, Pallas kernels, per_device(): pl.pallas_call(functools.partial(ladder_kernel, (slow, fast, n_vc, tiles,...  57 us
    unnamed x1, local copies, waits for them, and re-layouts  1.47 us

profile of v3, /device:TPU:1, one launch (start us, length us, event | category | flops | bytes accessed | tf_op | source)
XLA Modules:
  0.0 59.1 jit_solution(13915011723377681459)
XLA Ops:
  0.7 57.0 %ladder.1 = bf16[16,2048]{1,0:T(8,128)(2,1)} custom-call(s32[1]{0:T(128)S(6)} %copy.7.count_ref, s32[2,256]{1,0:T(2,128)} %bitcast.7, bf16[100,16,128]{2,1,0:T(8,128)(2,1)} %bitcast.6, bf16[256,128,128]{2,1,0:T(8,128)(2,1)} %tiles_hbm.1), custom_call_target="tpu_custom_call" | custom-call | tf_op jit(solution)/shard_map/ladder/pallas_call | solution.py:467
  57.6 1.5 %copy.8 = bf16[16,2048]{1,0:T(8,128)(2,1)} copy(bf16[16,2048]{1,0:T(8,128)(2,1)} %ladder.1) | data formatting | bytes 131072

commit v4 on v3

--- a/solution.py
+++ b/solution.py
@@ -187,17 +187,16 @@
             if side:
                 sideways(a + far, k)
 
-    for first, last, side in ((0, own_chunks, True), (own_chunks, chunks, False)):
-        if first == last:
-            continue
-
+    phases = [(first, last, side) for first, last, side in
+              ((0, own_chunks, True), (own_chunks, chunks, False)) if first < last]
+    for first, last, side in phases:
         def own(k, carry, side=side):
             own_chunk(k, side)
             return carry
 
         lax.fori_loop(first, last, own, 0)
-        if first == 0:
-            meanwhile()
+    meanwhile()
+    for first, last, side in phases:
         for far in range(1, slow if side else slow - 1):
             def passed(k, carry, far=far, side=side):
                 passed_chunk(far, k, side)

time: 59.3 us -> 57.2 us (0.965)
  the two profiles are of different devices: /device:TPU:1 before, /device:TPU:24 now
where the time goes in v4:
time: 57.2 us; the launch traced here: 57 us
  Pallas kernels  54.9 us (96%)
  local copies, waits for them, and re-layouts  1.47 us (3%)
  between operations  0.66 us (1%)
    pallas_call x1, Pallas kernels, per_device(): pl.pallas_call(functools.partial(ladder_kernel, (slow, fast, n_vc, tiles,...  54.9 us
    unnamed x1, local copies, waits for them, and re-layouts  1.47 us

profile of v4, /device:TPU:24, one launch (start us, length us, event | category | flops | bytes accessed | tf_op | source)
XLA Modules:
  0.0 57.0 jit_solution(14722895807390826710)
XLA Ops:
  0.7 54.9 %ladder.1 = bf16[16,2048]{1,0:T(8,128)(2,1)} custom-call(s32[1]{0:T(128)S(6)} %copy.7.count_ref, s32[2,256]{1,0:T(2,128)} %bitcast.7, bf16[100,16,128]{2,1,0:T(8,128)(2,1)} %bitcast.6, bf16[256,128,128]{2,1,0:T(8,128)(2,1)} %tiles_hbm.1), custom_call_target="tpu_custom_call" | custom-call | tf_op jit(solution)/shard_map/ladder/pallas_call | solution.py:466
  55.6 1.5 %copy.8 = bf16[16,2048]{1,0:T(8,128)(2,1)} copy(bf16[16,2048]{1,0:T(8,128)(2,1)} %ladder.1) | data formatting | bytes 131072

commit v5 on v4

--- a/solution.py
+++ b/solution.py
@@ -459,7 +459,7 @@
     at_once = early_rows if early_rows <= 64 else min(plane_rows, 64)
     slots_batch = largest_divisor(slots, 16)
     outer = n_vc // PAIR
-    parts = largest_divisor(AB_TILES, 4)
+    parts = largest_divisor(AB_TILES, 2)
     block = (AB_TILES, out_rows, width)
     dma = pltpu.SemaphoreType.DMA
     in_smem = pl.BlockSpec(memory_space=pltpu.SMEM)

time: 57.2 us -> 57.1 us (level)
  no operation moved by 1% of the time
where the time goes in v5:
time: 57.1 us; the launch traced here: 57 us
  Pallas kernels  54.8 us (96%)
  local copies, waits for them, and re-layouts  1.47 us (3%)
  between operations  0.66 us (1%)
    pallas_call x1, Pallas kernels, per_device(): pl.pallas_call(functools.partial(ladder_kernel, (slow, fast, n_vc, tiles,...  54.8 us
    unnamed x1, local copies, waits for them, and re-layouts  1.47 us

profile of v5, /device:TPU:24, one launch (start us, length us, event | category | flops | bytes accessed | tf_op | source)
XLA Modules:
  0.0 57.0 jit_solution(609671492827657571)
XLA Ops:
  0.7 54.8 %ladder.1 = bf16[16,2048]{1,0:T(8,128)(2,1)} custom-call(s32[1]{0:T(128)S(6)} %copy.7.count_ref, s32[2,256]{1,0:T(2,128)} %bitcast.7, bf16[100,16,128]{2,1,0:T(8,128)(2,1)} %bitcast.6, bf16[256,128,128]{2,1,0:T(8,128)(2,1)} %tiles_hbm.1), custom_call_target="tpu_custom_call" | custom-call | tf_op jit(solution)/shard_map/ladder/pallas_call | solution.py:466
  55.5 1.5 %copy.8 = bf16[16,2048]{1,0:T(8,128)(2,1)} copy(bf16[16,2048]{1,0:T(8,128)(2,1)} %ladder.1) | data formatting | bytes 131072
